TPU v7x, 256 devices: a whole 4x4x8 slice. The times are simulated.
256 devices in a mesh: ctx: 16 (over x, y), vis: 16 (over z, core).
Axes of the slice: x: 4, y: 4, z: 8, core: 2. Of those that a mesh axis runs over, the one named last changes fastest.
Arguments:
- patches: bfloat16 [32768, 1280], P(('ctx', 'vis')), may hold values from -10 to 10
- vis_gain: float32 [1280], replicated, may hold values from 0.5 to 1.5
- w_qkv: bfloat16 [1280, 3840], P(None, 'vis'), may hold values from -2 to 2
- w_out: bfloat16 [1280, 1280], P('vis'), may hold values from -0.15625 to 0.15625
- merge_gain: float32 [1280], replicated, may hold values from 0.5 to 1.5
- w_merge: bfloat16 [5120, 8192], P(None, 'vis'), may hold values from -0.078125 to 0.078125
- token_dest: int32 [16, 512], replicated, may hold values from 0 to 15, as said below
- token_row: int32 [16, 512], replicated, may hold values from 0 to 1023, as said below
- prompt_text: bfloat16 [16384, 8192], P('ctx', 'vis'), may hold values from -6 to 6
- kv_gain: float32 [8192], P('vis'), may hold values from 0.5 to 1.5
- w_kv: bfloat16 [8192, 1024], P('vis'), may hold values from -1 to 1
- queries: bfloat16 [2048, 4096], P('ctx'), may hold values from -12 to 12
- resp_kv: bfloat16 [2048, 1024], P('ctx'), may hold values from -12 to 12
- resp_len: int32 [16], P('ctx'), may hold values from 64 to 128
Outputs:
- attended: bfloat16 [2048, 4096], P('ctx')
Inputs may be any that keep to these rules, and one draw needn't show every extreme that they name: `token_dest`: the tokens of one image are in order of their prompt shard; at most 48 tokens of one image go to one shard, and from every image exactly 48 go to some shard. `token_row`: no two visual tokens take the same position of one shard.
All inputs are finite; a program needn't handle non-finite values.
Results may differ from a plain program's by a relative error of at most 0.014.
Values may be sent and summed in bfloat16 or wider, within the bound.
No kernel may reach another device: no remote copies, remote signals or barrier semaphores. Data moves between devices by JAX's collectives and lax.ppermute only.
A program may use at most 128 MiB of HBM per device.

v0:
```python
import math

import jax
import jax.numpy as jnp
from jax import lax
from jax.sharding import PartitionSpec as P

VD = 1280
VHEADS = 16
D = 8192
HD = 128
QH = 32
KVH = 4
VHD = 80
MD = 5120


EPS = 1e-06


def merged_2(shard, axis, combine):
    everything = jax.tree.map(lambda part: lax.all_gather(part, axis), shard)
    initial = jax.tree.map(lambda part: part[0], everything)

    def lap(k, so_far):
        return combine(so_far, jax.tree.map(lambda part: part[k], everything))

    return lax.fori_loop(1, lax.axis_size(axis), lap, initial)


def layer_norm(values, gain):
    center = values - jnp.mean(values, axis=-1, keepdims=True)
    spread = jnp.mean(center * center, axis=-1, keepdims=True)
    return center * lax.rsqrt(spread + EPS) * gain


def dense_attention(query, keys, values):
    count = query.shape[0]
    block = min(512, count)
    scale = 1.0 / math.sqrt(query.shape[1])

    def one_block(part):
        scores = jnp.dot(part, keys.T, preferred_element_type=jnp.float32) * scale
        highest = jnp.max(scores, axis=1, keepdims=True)
        expo = jnp.exp(scores - highest)
        summed = jnp.sum(expo, axis=1, keepdims=True)
        mixed = jnp.dot(expo.astype(jnp.bfloat16), values, preferred_element_type=jnp.float32)
        return (mixed / summed).astype(jnp.bfloat16)

    blocks = query.reshape(count // block, block, query.shape[1])
    return lax.map(one_block, blocks).reshape(count, values.shape[1])


def head_attention(packed):
    stacked = jnp.transpose(packed, (1, 0, 2))

    def one_head(item):
        return dense_attention(item[:, :VHD], item[:, VHD : 2 * VHD], item[:, 2 * VHD :])

    return jnp.transpose(lax.map(one_head, stacked), (1, 0, 2))


def grouped_attention(block):
    image_rows = block.shape[0]
    head_count = block.shape[2]
    result = head_attention(block.reshape(image_rows, head_count, 3 * VHD))
    return result.reshape(image_rows, 1, head_count, VHD)


def combine_partial(first, second):
    highest = jnp.maximum(first[0], second[0])
    fade_one = jnp.exp(first[0] - highest)
    fade_two = jnp.exp(second[0] - highest)
    return (
        highest,
        first[1] * fade_one + second[1] * fade_two,
        first[2] * fade_one[..., None] + second[2] * fade_two[..., None],
    )


def per_device(
    patches,
    vis_gain,
    w_qkv,
    w_out,
    merge_gain,
    w_merge,
    token_dest,
    token_row,
    prompt_text,
    kv_gain,
    w_kv,
    queries,
    resp_kv,
    resp_len,
):
    ctx_count = lax.axis_size("ctx")
    vis_count = lax.axis_size("vis")
    ctx_index = lax.axis_index("ctx")
    vis_index = lax.axis_index("vis")
    patch_count = patches.shape[0]
    floats = patches.astype(jnp.float32)
    normed = layer_norm(floats, vis_gain).astype(jnp.bfloat16)
    local_heads = VHEADS // vis_count
    qkv = jnp.dot(
        normed, lax.all_gather(w_qkv, "vis", axis=1, tiled=True), preferred_element_type=jnp.float32
    ).astype(jnp.bfloat16)
    packed = qkv.reshape(patch_count, vis_count, local_heads, 3 * VHD)
    grouped = grouped_attention(
        lax.all_to_all(packed, "vis", split_axis=1, concat_axis=0, tiled=True)
    )
    heads = grouped.reshape(grouped.shape[0], local_heads, VHD)
    returned = lax.all_to_all(heads, "vis", split_axis=0, concat_axis=1, tiled=True).reshape(
        patch_count, VD
    )
    projected = jnp.dot(
        returned,
        lax.all_gather(w_out, "vis", axis=0, tiled=True),
        preferred_element_type=jnp.float32,
    )
    mixed = floats + projected
    merged = layer_norm(mixed, merge_gain).astype(jnp.bfloat16).reshape(patch_count // 4, MD)
    visual = jnp.dot(
        lax.all_gather(merged, "vis", axis=0, tiled=True),
        w_merge,
        preferred_element_type=jnp.float32,
    ).astype(jnp.bfloat16)
    image_tokens = visual.shape[0]
    capacity = 3 * (image_tokens // ctx_count) // 2
    slots = jnp.arange(capacity, dtype=jnp.int32)
    shard_rows = prompt_text.shape[0]
    own_dest = lax.dynamic_index_in_dim(token_dest, ctx_index, 0, keepdims=False)
    shards = jnp.arange(ctx_count, dtype=jnp.int32)
    counts_out = jnp.sum((own_dest[None, :] == shards[:, None]).astype(jnp.int32), axis=1)
    starts_out = jnp.cumsum(counts_out) - counts_out
    picks = jnp.clip(starts_out[:, None] + slots[None, :], 0, image_tokens - 1).reshape(-1)
    filled = (slots[None, :] < counts_out[:, None]).reshape(-1, 1)
    outgoing = jnp.take(visual, picks, axis=0)
    outgoing = jnp.where(filled, outgoing, jnp.zeros_like(outgoing)).reshape(
        ctx_count, capacity, -1
    )
    arrived = lax.all_to_all(outgoing, "ctx", split_axis=0, concat_axis=0, tiled=True)
    pool = arrived.reshape(ctx_count * capacity, -1)
    firsts = jnp.sum((token_dest < ctx_index).astype(jnp.int32), axis=1)
    counts_in = jnp.sum((token_dest == ctx_index).astype(jnp.int32), axis=1)
    lookup = jnp.clip(firsts[:, None] + slots[None, :], 0, image_tokens - 1)
    places = jnp.take_along_axis(token_row, lookup, axis=1)
    live = slots[None, :] < counts_in[:, None]
    targets = jnp.where(live, places, shard_rows).reshape(-1)
    numbers = jnp.arange(ctx_count * capacity, dtype=jnp.int32) + 1
    source = jnp.zeros((shard_rows,), jnp.int32).at[targets].set(numbers, mode="drop")
    incoming = jnp.take(pool, jnp.maximum(source - 1, 0), axis=0)
    prompt = jnp.where((source > 0)[:, None], incoming, prompt_text)
    prompt_floats = prompt.astype(jnp.float32)
    squares = lax.psum(jnp.sum(prompt_floats * prompt_floats, axis=1), "vis")
    inverse = lax.rsqrt(squares / D + EPS)
    scaled = (prompt_floats * inverse[:, None] * kv_gain).astype(jnp.bfloat16)
    kv_share = lax.psum_scatter(
        jnp.dot(scaled, w_kv, preferred_element_type=jnp.float32),
        "vis",
        scatter_dimension=0,
        tiled=True,
    ).astype(jnp.bfloat16)
    width = KVH * HD
    group = QH // KVH
    resp_rows = queries.shape[0]
    scale = 1.0 / math.sqrt(HD)
    q_heads = queries.reshape(resp_rows, KVH, group, HD)

    def update(state, keys, values, visible):
        highest, summed, weighted = state
        scores = (
            jnp.einsum("rkgd,nkd->kgrn", q_heads, keys, preferred_element_type=jnp.float32) * scale
        )
        if visible is not None:
            scores = jnp.where(visible, scores, -1e30)
        new_high = jnp.maximum(highest, jnp.max(scores, axis=3))
        expo = jnp.exp(scores - new_high[..., None])
        if visible is not None:
            expo = jnp.where(visible, expo, 0.0)
        fade = jnp.exp(highest - new_high)
        summed = summed * fade + jnp.sum(expo, axis=3)
        weighted = weighted * fade[..., None] + jnp.einsum(
            "kgrn,nkd->kgrd", expo.astype(jnp.bfloat16), values, preferred_element_type=jnp.float32
        )
        return (new_high, summed, weighted)

    def fold_block(state, piece):
        count = piece.shape[0]
        return update(
            state,
            piece[:, :width].reshape(count, KVH, HD),
            piece[:, width:].reshape(count, KVH, HD),
            None,
        )

    own_count = resp_rows // vis_count
    own = lax.dynamic_slice_in_dim(resp_kv, vis_index * own_count, own_count, 0)
    key_positions = vis_index * own_count + jnp.arange(own_count, dtype=jnp.int32)
    query_positions = jnp.arange(resp_rows, dtype=jnp.int32)
    own_visible = key_positions[None, :] <= query_positions[:, None]
    start_state = (
        jnp.full((KVH, group, resp_rows), -1e30, jnp.float32),
        jnp.zeros((KVH, group, resp_rows), jnp.float32),
        jnp.zeros((KVH, group, resp_rows, HD), jnp.float32),
    )
    state = update(
        start_state,
        own[:, :width].reshape(own_count, KVH, HD),
        own[:, width:].reshape(own_count, KVH, HD),
        own_visible,
    )
    fold_state = state
    piece = lax.all_gather(kv_share, "ctx", axis=0, tiled=True)
    count = piece.shape[0]
    blocks = piece.reshape(count // 512, 512, 2 * width)

    def scan_step(inner, block):
        return (fold_block(inner, block), None)

    fold_state, unused = lax.scan(scan_step, fold_state, blocks)
    state = fold_state
    highest, summed, weighted = merged_2(state, "vis", combine_partial)
    result = weighted / summed[..., None]
    result = jnp.transpose(result, (2, 0, 1, 3)).reshape(resp_rows, QH * HD)
    live = (query_positions < resp_len[0])[:, None]
    return jnp.where(live, result, 0.0).astype(jnp.bfloat16)


def solution(mesh):
    return jax.shard_map(
        per_device,
        mesh=mesh,
        in_specs=(
            P(("ctx", "vis"), None),
            P(),
            P(None, "vis"),
            P("vis", None),
            P(),
            P(None, "vis"),
            P(),
            P(),
            P("ctx", "vis"),
            P("vis"),
            P("vis", None),
            P("ctx", None),
            P("ctx", None),
            P("ctx"),
        ),
        out_specs=P("ctx", None),
        check_vma=False,
    )
```

profile of v0, /device:TPU:1, one launch (start us, length us, event | category | flops | bytes accessed | tf_op | source)
XLA Modules:
  0.0 634.2 jit_solution(6162034617860359859)
XLA Ops:
  9.6 66.6 %all-gather.9.cloned.1.call-done = bf16[1280,3840]{0,1:T(8,128)(2,1)} async-done(((bf16[1280,240]{0,1:T(8,128)(2,1)}), bf16[1280,3840]{0,1:T(8,128)(2,1)}) %all-gather.9.cloned.1.call-update) | async-done | bytes 9830416 | tf_op jit(solution)/shard_map/all_gather | solution.py:106
  76.1 7.3 %convolution_convert_fusion = bf16[128,3840]{1,0:T(8,128)(2,1)S(1)} fusion(bf16[1280,3840]{0,1:T(8,128)(2,1)} %all-gather.9.cloned.1.call-done, bf16[128,1280]{1,0:T(8,128)(2,1)} %param.20, f32[1280]{0:T(1024)} %param.21, f32[128]{0:T(128)S(1)} %add_rsqrt_fusion.2, f32[128]{0:T(128)S(1)} %broadcast_multiply_fusion.1), kind=kOutput, calls=%fused_computation.41 | convolution fusion | flops 1259601920 | bytes 11147264 | tf_op jit(solution)/shard_map/dot_general | solution.py:105
  84.7 4.5 all-to-all-start
  90.2 28.3 %all-to-all-done = bf16[128,16,1,240]{0,3,2,1:T(8,128)(2,1)S(1)} async-done(((bf16[128,16,1,240]{0,3,2,1:T(8,128)(2,1)}), bf16[128,16,1,240]{0,3,2,1:T(8,128)(2,1)S(1)}, u32[]{:S(2)}, u32[]{:S(2)}) %all-to-all-start) | async-done | bytes 983072 | tf_op jit(solution)/shard_map/all_to_all | solution.py:110
  120.0 10.5 %while.50 = (s32[]{:T(128)}, bf16[4,512,80]{1,2,0:T(8,128)(2,1)S(1)}, bf16[4,512,80]{2,1,0:T(8,128)(2,1)S(1)}, bf16[2048,80]{1,0:T(8,128)(2,1)S(1)}, bf16[2048,80]{1,0:T(8,128)(2,1)S(1)}, /*index=5*/s32[]{:T(128)}) while((s32[]{:T(128)}, bf16[4,512,80]{1,2,0:T(8,128)(2,1)S(1)}, bf16[4,512,80]{2,1,0:T(8,128)(2,1)S(1)}, ...), condition=%wide.region_12.13_spmd, body=%wide.region_9.12_spmd.sunk | while | flops 344013824 | bytes 13854797 | solution.py:51
  131.6 11.5 %reduce.5 = bf16[2048,80]{1,0:T(8,128)(2,1)S(1)} reduce(bf16[2048,1,80]{2,1,0:T(2,128)(2,1)S(1)} %reshape.393, bf16[]{:T(256)} %broadcast.386), dimensions={1}, to_apply=%reshape.393.reduce_sub_computation | reduce | bytes 655362 | tf_op jit(solution)/shard_map/transpose | solution.py:60
  144.2 17.1 %all_to_all.35 = bf16[16,2,5120]{2,1,0:T(2,128)(2,1)S(1)} all-to-all(bf16[16,2,5120]{2,1,0:T(2,128)(2,1)S(1)} %reshape.399), channel_id=1, replica_groups=mesh['ctx'=16,'vis'=16] {'vis'}, dimensions={0} | all-to-all | bytes 655360 | tf_op jit(solution)/shard_map/all_to_all | solution.py:113
  168.2 39.6 %all-gather.13.cloned.1.call-done = bf16[512,5120]{1,0:T(8,128)(2,1)} async-done(((bf16[32,5120]{1,0:T(8,128)(2,1)}), bf16[512,5120]{1,0:T(8,128)(2,1)}) %all-gather.13.cloned.1.call-update) | async-done | bytes 5242896 | tf_op jit(solution)/shard_map/all_gather | solution.py:124
  207.8 6.9 %convolution_convert_fusion.1 = bf16[512,512]{1,0:T(8,128)(2,1)S(1)} fusion(bf16[512,5120]{1,0:T(8,128)(2,1)} %all-gather.13.cloned.1.call-done, bf16[5120,512]{1,0:T(8,128)(2,1)} %param.25), kind=kOutput, calls=%fused_computation.52 | convolution fusion | flops 2684616704 | bytes 11010048 | tf_op jit(solution)/shard_map/dot_general | solution.py:123
  218.6 6.5 %all-to-all-start.2 = ((bf16[16,48,512]{2,1,0:T(8,128)(2,1)}), bf16[16,48,512]{2,1,0:T(8,128)(2,1)S(1)}, u32[]{:S(2)}, u32[]{:S(2)}) async-start(bf16[16,48,512]{2,1,0:T(8,128)(2,1)} %select_select_fusion.1), calls=%async_computation.2 | async-start | bytes 1572864 | tf_op jit(solution)/shard_map/all_to_all | solution.py:142
  225.6 6.3 gather_fusion.2
  232.0 3.4 scatter_custom_fusion
  237.7 4.0 gather_fusion.1
  241.7 2.8 fusion.36
  244.5 25.8 %psum.7 = f32[1024]{0:T(1024)S(1)} all-reduce(f32[1024]{0:T(1024)S(1)} %get-tuple-element.341), channel_id=1, replica_groups=mesh['ctx'=16,'vis'=16] {'vis'}, use_global_device_ids=true, to_apply=%region_16.17 | all-reduce | flops 1024 | bytes 8192 | tf_op jit(solution)/shard_map/psum | solution.py:155
  270.3 4.5 fusion.42
  274.8 55.9 %reduce-scatter.2.cloned.1.call-done = f32[64,1024]{1,0:T(8,128)} async-done(((f32[1024,1024]{1,0:T(8,128)}), f32[64,1024]{1,0:T(8,128)}) %reduce-scatter.2.cloned.1.call-update) | async-done | bytes 262160 | tf_op jit(solution)/shard_map/reduce_scatter | solution.py:158
  338.5 45.2 %all-gather.15.cloned.1.call-done = bf16[1024,1024]{1,0:T(8,128)(2,1)} async-done(((bf16[64,1024]{1,0:T(8,128)(2,1)}), bf16[1024,1024]{1,0:T(8,128)(2,1)}) %all-gather.15.cloned.1.call-update) | async-done | bytes 2097168 | tf_op jit(solution)/shard_map/all_gather | solution.py:214
  383.8 20.4 %while.51 = (s32[]{:T(128)}, f32[4,8,128]{2,1,0:T(8,128)S(1)}, f32[4,8,128]{2,1,0:T(8,128)S(1)}, f32[4,8,128,128]{3,2,1,0:T(8,128)}, bf16[2,512,1024]{2,1,0:T(8,...) while((s32[]{:T(128)}, f32[4,8,128]{2,1,0:T(8,128)S(1)}, f32[4,8,128]{2,1,0:T(8,128)S(1)}, ...), condition=%wide.region_21.22_spmd, body=%wide.region_18.21_spmd.sunk | while | flops 1091575808 | bytes 54788232 | solution.py:221
  400.1 2.8 multiply_add_fusion.5
  404.9 19.9 %all-gather = f32[64,8,128]{2,1,0:T(8,128)S(1)} all-gather(f32[4,8,128]{2,1,0:T(8,128)S(1)} %get-tuple-element.253), channel_id=2, replica_groups=mesh['ctx'=16,'vis'=16] {'vis'}, dimensions={0}, use_global_device_ids=true | all-gather | bytes 278528 | tf_op jit(solution)/shard_map/all_gather | solution.py:22
  424.8 16.9 %all-gather.1 = f32[64,8,128]{2,1,0:T(8,128)S(1)} all-gather(f32[4,8,128]{2,1,0:T(8,128)S(1)} %get-tuple-element.254), channel_id=3, replica_groups=mesh['ctx'=16,'vis'=16] {'vis'}, dimensions={0}, use_global_device_ids=true | all-gather | bytes 278528 | tf_op jit(solution)/shard_map/all_gather | solution.py:22
  441.7 139.5 %all-gather.17.cloned.1.call-done = f32[64,8,128,128]{3,2,1,0:T(8,128)} async-done(((f32[4,8,128,128]{3,2,1,0:T(8,128)}), f32[64,8,128,128]{3,2,1,0:T(8,128)}) %all-gather.17.cloned.1.call-update) | async-done | bytes 33554448 | tf_op jit(solution)/shard_map/all_gather | solution.py:22
  582.9 41.5 %while.52 = (s32[]{:T(128)}, f32[4,8,128]{2,1,0:T(8,128)S(1)}, f32[4,8,128]{2,1,0:T(8,128)S(1)}, f32[4,8,128,128]{3,2,1,0:T(8,128)S(1)}, f32[16,4,8,128]{3,2,1,0...) while((s32[]{:T(128)}, f32[4,8,128]{2,1,0:T(8,128)S(1)}, ...), condition=%wide.region_23.24_spmd, body=%wide.region_22.23_spmd.sunk | while | flops 1597445 | bytes 6455447 | solution.py:28
  (167 shorter events, 103.6 us)
Async XLA Ops:
  6.5 263.8 %copy-start = (bf16[512,1024]{1,0:T(8,128)(2,1)S(1)}, bf16[512,1024]{1,0:T(8,128)(2,1)}, u32[]{:S(2)}) copy-start(bf16[512,1024]{1,0:T(8,128)(2,1)} %param.30) | copy-start | bytes 3145732
  6.5 69.6 %all-gather.9.cloned.1.call-start = ((), (), s32[]{:S(2)}) async-start(), calls=%async_computation.4 | async-start | bytes 10444800 | tf_op jit(solution)/shard_map/all_gather | solution.py:106
  84.7 33.8 %all-to-all-start = ((bf16[128,16,1,240]{0,3,2,1:T(8,128)(2,1)}), bf16[128,16,1,240]{0,3,2,1:T(8,128)(2,1)S(1)}, u32[]{:S(2)}, u32[]{:S(2)}) async-start(bf16[128,16,1,240]{0,3,2,1:T(8,128)(2,1)} %bitcast.23), calls=%async_computation | async-start | bytes 1966080 | tf_op jit(solution)/shard_map/all_to_all | solution.py:110
  89.2 74.0 %all-gather.11.cloned.1.call-start = ((), (), s32[]{:S(2)}) async-start(), calls=%async_computation.5 | async-start | bytes 3481600 | tf_op jit(solution)/shard_map/all_gather | solution.py:118
  90.0 117.8 %all-gather.13.cloned.1.call-start = ((), (), s32[]{:S(2)}) async-start(), calls=%async_computation.6 | async-start | bytes 5570560 | tf_op jit(solution)/shard_map/all_gather | solution.py:124
  130.8 32.5 %copy-start.5 = (bf16[128,1280]{1,0:T(8,128)(2,1)S(1)}, bf16[128,1280]{1,0:T(8,128)(2,1)}, u32[]{:S(2)}) copy-start(bf16[128,1280]{1,0:T(8,128)(2,1)} %param.20) | copy-start | bytes 983044
  162.4 3.7 copy-start.8
  163.1 4.2 copy-start.7
  214.7 10.9 %copy-start.2 = (s32[16,512]{1,0:T(8,128)S(1)}, s32[16,512]{1,0:T(8,128)}, u32[]{:S(2)}) copy-start(s32[16,512]{1,0:T(8,128)} %param.27) | copy-start | bytes 98308
  218.6 19.2 %all-to-all-start.2 = ((bf16[16,48,512]{2,1,0:T(8,128)(2,1)}), bf16[16,48,512]{2,1,0:T(8,128)(2,1)S(1)}, u32[]{:S(2)}, u32[]{:S(2)}) async-start(bf16[16,48,512]{2,1,0:T(8,128)(2,1)} %select_select_fusion.1), calls=%async_computation.2 | async-start | bytes 1572864 | tf_op jit(solution)/shard_map/all_to_all | solution.py:142
  225.1 105.6 %reduce-scatter.2.cloned.1.call-start = ((), (), s32[]{:S(2)}) async-start(), calls=%async_computation.7 | async-start | bytes 4456448 | tf_op jit(solution)/shard_map/reduce_scatter | solution.py:158
  237.7 32.6 %copy-start.9 = (f32[512]{0:T(512)S(1)}, f32[512]{0:T(512)}, u32[]{:S(2)}) copy-start(f32[512]{0:T(512)} %param.29) | copy-start | bytes 6148
  274.8 57.9 %copy-start.6 = (bf16[128,4096]{1,0:T(8,128)(2,1)S(1)}, bf16[128,4096]{1,0:T(8,128)(2,1)}, u32[]{:S(2)}) copy-start(bf16[128,4096]{1,0:T(8,128)(2,1)} %param.31) | copy-start | bytes 3145732
  274.8 109.0 %all-gather.15.cloned.1.call-start = ((), (), s32[]{:S(2)}) async-start(), calls=%async_computation.8 | async-start | bytes 2228224 | tf_op jit(solution)/shard_map/all_gather | solution.py:214
  332.3 248.9 %all-gather.17.cloned.1.call-start = ((), (), s32[]{:S(2)}) async-start(), calls=%async_computation.9 | async-start | bytes 35651584 | tf_op jit(solution)/shard_map/all_gather | solution.py:22
  388.3 1.6 copy-start.3
  392.7 1.3 copy-start.4
  398.5 1.6 copy-start.3
  402.9 1.3 copy-start.4
  624.4 2.9 copy-start.1
Sparse Core Ops, SparseCore 0:
  9.2 66.9 all-gather.8
  91.9 48.2 all-gather.10
  167.4 40.3 all-gather.12
  274.9 55.7 reduce-scatter.1
  333.0 50.7 all-gather.14
  404.4 176.8 all-gather.16
where the time goes:
time: 635 us; the launch traced here: 634 us
  waiting for transfers between devices  379 us (60%)
  blocking collectives  79.8 us (13%)
  other arithmetic  70.4 us (11%)
  matrix products  42.8 us (7%)
  local copies, waits for them, and re-layouts  35.3 us (6%)
  between operations  14.6 us (2%)
  starting transfers between devices  11.7 us (2%)
    all_gather x1, waiting for transfers between devices, merged_2(): everything = jax.tree.map(lambda part: lax.all_gather(part, axis), shard)  139 us
    all_gather x1, waiting for transfers between devices, per_device(): lax.all_gather(w_qkv, 'vis', axis=1, tiled=True)  66.6 us
    reduce_scatter x1, waiting for transfers between devices, per_device(): lax.psum_scatter(jnp.dot(scaled, w_kv, preferred_element_type=jnp.float32...  55.9 us
    all_gather x1, waiting for transfers between devices, per_device(): piece = lax.all_gather(kv_share, 'ctx', axis=0, tiled=True)  45.2 us
    add x15, other arithmetic, combine_partial(): first[2] * fade_one[..., None] + second[2] * fade_two[..., None]  40.6 us
    all_gather x1, waiting for transfers between devices, per_device(): lax.all_gather(merged, 'vis', axis=0, tiled=True)  39.6 us
    all_gather x2, blocking collectives, merged_2(): everything = jax.tree.map(lambda part: lax.all_gather(part, axis), shard)  36.8 us
    all_to_all x1, waiting for transfers between devices, per_device(): lax.all_to_all(packed, 'vis', split_axis=1, concat_axis=0, tiled=True)  28.3 us
  transfers between devices with their start and end apart: 8, of which 7 were waited for; matrix products, arithmetic and copies ran while one was open for 7% of the time, Pallas kernels for 0%

commit v1 on v0

v1 whole, which is shorter than its diff:
```python
import math

import jax
import jax.numpy as jnp
from jax import lax
from jax.experimental import pallas as pl
from jax.experimental.pallas import tpu as pltpu
from jax.sharding import PartitionSpec as P

VD = 1280
VHEADS = 16
D = 8192
HD = 128
QH = 32
KVH = 4
CROWS = 1024
R_TOK = 128
VHD = 80
GP = 2048
VTOK = 512
N = 16
LOCAL = GP // N
EPS = 1e-06
NEG = -1e30
bf16 = jnp.bfloat16
f32 = jnp.float32

SWAP = [(i, i ^ 1) for i in range(N)]
QUADS = [[4 * g + i for i in range(4)] for g in range(4)]
RING_ORDER = (0, 1, 2, 3, -1, -2, -3, 4)


def along_z(shift):
    return [(z * 2 + c, ((z + shift) % 8) * 2 + c) for z in range(8) for c in range(2)]


def ring_gather(block):
    ups = [block]
    downs = [block]
    for step in range(1, 4):
        ups.append(lax.ppermute(ups[-1], "vis", along_z(1)))
        downs.append(lax.ppermute(downs[-1], "vis", along_z(-1)))
    half = block.shape[0] // 2
    up = lax.ppermute(ups[-1][:half], "vis", along_z(1))
    down = lax.ppermute(downs[-1][half:], "vis", along_z(-1))
    mine = jnp.concatenate(ups + downs[1:] + [up, down], axis=0)
    return jnp.concatenate([mine, lax.ppermute(mine, "vis", SWAP)], axis=0)


def ring_owners(vis_index):
    z = vis_index // 2
    core = vis_index % 2
    zs = (z - jnp.array(RING_ORDER, jnp.int32)) % 8
    return jnp.concatenate([zs * 2 + core, zs * 2 + 1 - core])


def dot(a, b, contract):
    return lax.dot_general(a, b, ((contract[:1], contract[1:]), ((), ())), preferred_element_type=f32)


def normed_rows(values, gain):
    center = values - jnp.mean(values, axis=-1, keepdims=True)
    spread = jnp.mean(center * center, axis=-1, keepdims=True)
    return center * lax.rsqrt(spread + EPS) * gain


QKV_STEPS = 4
QKV_ROWS = GP // QKV_STEPS
ATT_STEPS = 8
ATT_ROWS = GP // ATT_STEPS


def vision_kernel(x_ref, gain_ref, w_ref, out_ref, q_s, k_s, v_s):
    step = pl.program_id(0)

    @pl.when(step < QKV_STEPS)
    def _():
        normed = normed_rows(x_ref[...].astype(f32), gain_ref[...]).astype(bf16)
        qkv = dot(normed, w_ref[...], (1, 0)).astype(bf16)
        rows = pl.ds(pl.multiple_of(step * QKV_ROWS, QKV_ROWS), QKV_ROWS)
        q_s[rows, :] = qkv[:, :128]
        k_s[rows, :] = qkv[:, 128:256]
        v_s[rows, :] = qkv[:, 256:]

    @pl.when(step >= QKV_STEPS)
    def _():
        first = pl.multiple_of((step - QKV_STEPS) * ATT_ROWS, ATT_ROWS)
        query = q_s[pl.ds(first, ATT_ROWS), :]
        scores = dot(query, k_s[...], (1, 1)) * (1.0 / math.sqrt(VHD))
        highest = jnp.max(scores, axis=1, keepdims=True)
        expo = jnp.exp(scores - highest)
        total = jnp.sum(expo, axis=1, keepdims=True)
        mixed = dot(expo.astype(bf16), v_s[...], (1, 0)) / total
        out_ref[...] = jnp.transpose(mixed, (1, 0))[:VHD, :].astype(bf16)


def vision(x, gain, w):
    return pl.pallas_call(
        vision_kernel,
        grid=(QKV_STEPS + ATT_STEPS,),
        in_specs=[
            pl.BlockSpec((QKV_ROWS, VD), lambda i: (jnp.minimum(i, QKV_STEPS - 1), 0)),
            pl.BlockSpec((1, VD), lambda i: (0, 0)),
            pl.BlockSpec((VD, 384), lambda i: (0, 0)),
        ],
        out_specs=pl.BlockSpec((VHD, ATT_ROWS), lambda i: (0, jnp.maximum(i - QKV_STEPS, 0))),
        out_shape=jax.ShapeDtypeStruct((VHD, GP), bf16),
        scratch_shapes=[pltpu.VMEM((GP, 128), bf16)] * 3,
        compiler_params=pltpu.CompilerParams(vmem_limit_bytes=40 * 2**20),
        name="vision",
    )(x, gain, w)


MERGE_STEPS = 4
MERGE_ROWS = GP // MERGE_STEPS
MERGE_TOK = VTOK // MERGE_STEPS
CHUNK = 72


def merge_kernel(order_ref, h_ref, x_ref, wo_ref, gain_ref, wm_ref, kg_ref, wk_ref, out_ref, wo_s):
    @pl.when(pl.program_id(0) == 0)
    def _():
        for k in range(N):
            wo_s[VHD * k : VHD * k + VHD, :] = wo_ref[order_ref[k]]

    mixed = x_ref[...].astype(f32) + dot(h_ref[...], wo_s[...], (0, 0))
    merged = normed_rows(mixed, gain_ref[...]).astype(bf16)
    pieces = merged.reshape(MERGE_ROWS // LOCAL, 4, LOCAL // 4, VD)
    visual = dot(pieces[:, 0].reshape(MERGE_TOK, VD), wm_ref[:VD, :], (1, 0))
    for a in range(1, 4):
        part = pieces[:, a].reshape(MERGE_TOK, VD)
        visual += dot(part, wm_ref[a * VD : (a + 1) * VD, :], (1, 0))
    visual = visual.astype(bf16).astype(f32)
    squares = jnp.sum(visual * visual, axis=1, keepdims=True)
    eye = lax.broadcasted_iota(jnp.int32, (MERGE_TOK, MERGE_TOK), 0) == lax.broadcasted_iota(
        jnp.int32, (MERGE_TOK, MERGE_TOK), 1
    )
    row = jnp.sum(jnp.where(eye, squares, 0.0), axis=0, keepdims=True)
    high = row.astype(bf16).astype(f32)
    middle = (row - high).astype(bf16).astype(f32)
    low = row - high - middle
    extra = jnp.concatenate([high, middle, low, jnp.zeros((5, MERGE_TOK), f32)], axis=0)
    gained = (visual * kg_ref[...]).astype(bf16)
    kv = dot(wk_ref[...], gained, (0, 1))
    for v in range(N):
        both = jnp.concatenate([kv[64 * v : 64 * v + 64, :], extra], axis=0)
        out_ref[v, :, :] = both.astype(bf16)


def merge(order, heads, x, w_out, gain, w_merge, kv_gain, w_kv):
    whole = lambda i, order: (0, 0)
    grid_spec = pltpu.PrefetchScalarGridSpec(
        num_scalar_prefetch=1,
        grid=(MERGE_STEPS,),
        in_specs=[
            pl.BlockSpec((VD, MERGE_ROWS), lambda i, order: (0, i)),
            pl.BlockSpec((MERGE_ROWS, VD), lambda i, order: (i, 0)),
            pl.BlockSpec((N, VHD, VD), lambda i, order: (0, 0, 0)),
            pl.BlockSpec((1, VD), whole),
            pl.BlockSpec((4 * VD, 512), whole),
            pl.BlockSpec((1, 512), whole),
            pl.BlockSpec((512, 1024), whole),
        ],
        out_specs=pl.BlockSpec((N, CHUNK, MERGE_TOK), lambda i, order: (0, 0, i)),
        scratch_shapes=[pltpu.VMEM((VD, VD), bf16)],
    )
    return pl.pallas_call(
        merge_kernel,
        grid_spec=grid_spec,
        out_shape=jax.ShapeDtypeStruct((N, CHUNK, VTOK), bf16),
        compiler_params=pltpu.CompilerParams(vmem_limit_bytes=56 * 2**20),
        name="merge",
    )(order, heads, x, w_out, gain, w_merge, kv_gain, w_kv)


PACK = 272


def response_kernel(qa_ref, qb_ref, text_ref, mask_ref, vis_ref, out_ref):
    qa = qa_ref[0]
    qb = qb_ref[0]
    query = jnp.concatenate([qa[:, :HD], qb[:, :HD], qa[:, HD:], qb[:, HD:]], axis=0)
    scale = 1.0 / math.sqrt(HD)
    first = dot(query, text_ref[:HD, :], (1, 0)) * scale + mask_ref[...]
    second = dot(query, vis_ref[:HD, :], (1, 0)) * scale
    highest = jnp.maximum(
        jnp.max(first, axis=1, keepdims=True), jnp.max(second, axis=1, keepdims=True)
    )
    first = jnp.exp(first - highest)
    second = jnp.exp(second - highest)
    total = jnp.sum(first, axis=1, keepdims=True) + jnp.sum(second, axis=1, keepdims=True)
    mixed = dot(first.astype(bf16), text_ref[HD:, :], (1, 1)) + dot(
        second.astype(bf16), vis_ref[HD:, :], (1, 1)
    )
    out_ref[0, : 2 * R_TOK, :] = (mixed / total).astype(bf16)
    level = highest + jnp.log(total)
    eye = lax.broadcasted_iota(jnp.int32, (256, 256), 0) == lax.broadcasted_iota(
        jnp.int32, (256, 256), 1
    )
    row = jnp.sum(jnp.where(eye, level, 0.0), axis=0, keepdims=True)
    high = row.astype(bf16).astype(f32)
    middle = (row - high).astype(bf16).astype(f32)
    low = row - high - middle
    parts = [part[:, k * 128 : k * 128 + 128] for part in (high, middle, low) for k in range(2)]
    tail = jnp.concatenate(parts + [jnp.zeros((10, 128), f32)], axis=0)
    out_ref[0, 2 * R_TOK :, :] = tail.astype(bf16)


def response(qa, qb, text, mask, vis):
    whole = lambda i: (0, 0)
    return pl.pallas_call(
        response_kernel,
        grid=(N,),
        in_specs=[
            pl.BlockSpec((1, R_TOK // 2, 2 * HD), lambda i: (i, 0, 0)),
            pl.BlockSpec((1, R_TOK // 2, 2 * HD), lambda i: (i, 0, 0)),
            pl.BlockSpec((2 * HD, CROWS), whole),
            pl.BlockSpec((1, CROWS), whole),
            pl.BlockSpec((2 * HD, VTOK), whole),
        ],
        out_specs=pl.BlockSpec((1, PACK, HD), lambda i: (i, 0, 0)),
        out_shape=jax.ShapeDtypeStruct((N, PACK, HD), bf16),
        compiler_params=pltpu.CompilerParams(vmem_limit_bytes=40 * 2**20),
        name="response",
    )(qa, qb, text, mask, vis)


def per_device(
    patches,
    vis_gain,
    w_qkv,
    w_out,
    merge_gain,
    w_merge,
    token_dest,
    token_row,
    prompt_text,
    kv_gain,
    w_kv,
    queries,
    resp_kv,
    resp_len,
):
    ctx_index = lax.axis_index("ctx")
    vis_index = lax.axis_index("vis")
    group = vis_index // 4

    local = patches.reshape(LOCAL // 4, 4, VD).transpose(1, 0, 2).reshape(LOCAL, VD)
    image = lax.all_gather(local, "vis", axis=0, tiled=True)

    own_q = lax.dynamic_slice_in_dim(queries, vis_index * 256, 256, 1)
    half = R_TOK // 2
    qa = lax.all_gather(own_q[:half], "ctx", axis=0)
    qb = lax.all_gather(own_q[half:], "ctx", axis=0)

    w_kv_mine = w_kv.reshape(512, 2, KVH, 2, 64).transpose(0, 2, 1, 3, 4).reshape(512, 1024)
    text = prompt_text.astype(f32)
    text_squares = jnp.sum(text * text, axis=1)
    text_gained = (text * kv_gain).astype(bf16)
    text_part = dot(w_kv_mine, text_gained, (0, 1)).reshape(N, 64, CROWS)
    text_extra = jnp.broadcast_to(text_squares[None, None, :], (N, 8, CROWS))
    text_part = jnp.concatenate([text_part, text_extra], axis=1).reshape(N * CHUNK, CROWS)

    flat_dest = token_dest.reshape(-1)
    flat_row = token_row.reshape(-1)
    here = jnp.where(flat_dest == ctx_index, flat_row // 128, -1)
    tall = (here[None, :] == jnp.arange(8, dtype=jnp.int32)[:, None]).astype(bf16)
    wide = ((flat_row % 128)[:, None] == jnp.arange(128, dtype=jnp.int32)[None, :]).astype(bf16)
    taken = dot(tall, wide, (1, 0)).reshape(1, CROWS)
    mask = jnp.where(taken > 0.5, NEG, 0.0)

    own_k = lax.dynamic_slice_in_dim(resp_kv, group * HD, HD, 1)
    own_v = lax.dynamic_slice_in_dim(resp_kv, KVH * HD + group * HD, HD, 1)
    positions = jnp.arange(R_TOK, dtype=jnp.int32)
    visible = positions[None, :] <= positions[:, None]
    q_two = own_q.reshape(R_TOK, 2, HD)
    own_scores = jnp.einsum("rhd,nd->hrn", q_two, own_k, preferred_element_type=f32)
    own_scores = jnp.where(visible, own_scores * (1.0 / math.sqrt(HD)), NEG)
    own_high = jnp.max(own_scores, axis=2, keepdims=True)
    own_expo = jnp.where(visible, jnp.exp(own_scores - own_high), 0.0)
    own_total = jnp.sum(own_expo, axis=2, keepdims=True)
    own_mixed = jnp.einsum("hrn,nd->hrd", own_expo.astype(bf16), own_v, preferred_element_type=f32)
    own_mixed = (own_mixed / own_total).reshape(256, HD)
    own_level = (own_high + jnp.log(own_total)).reshape(1, 256)

    image, qa, qb = lax.optimization_barrier((image, qa, qb))
    w_out, unused = lax.optimization_barrier((w_out, image[0, 0]))
    out_all = lax.all_gather(w_out, "vis", axis=0)
    out_all, text_part = lax.optimization_barrier((out_all, text_part))
    text_sum = lax.psum_scatter(text_part, "vis", scatter_dimension=0, tiled=True)
    text_scale = lax.rsqrt(text_sum[64:65] / D + EPS)
    text_kv = (text_sum[:64] * text_scale).astype(bf16)

    w_pad = jnp.pad(w_qkv.reshape(VD, 3, VHD), ((0, 0), (0, 0), (0, 128 - VHD))).reshape(VD, 384)
    heads = ring_gather(vision(image, vis_gain.reshape(1, VD), w_pad))
    partial = merge(
        ring_owners(vis_index),
        heads,
        image,
        out_all,
        merge_gain.reshape(1, VD),
        w_merge,
        kv_gain.reshape(1, 512),
        w_kv_mine,
    )
    arrived = lax.all_to_all(partial, "vis", split_axis=0, concat_axis=0, tiled=True)
    vis_sum = jnp.sum(arrived.astype(f32), axis=0)
    vis_squares = vis_sum[64:65] + vis_sum[65:66] + vis_sum[66:67]
    vis_kv = (vis_sum[:64] * lax.rsqrt(vis_squares / D + EPS)).astype(bf16)
    vis_kv = lax.all_gather(vis_kv, "vis", axis=0, tiled=True, axis_index_groups=QUADS)
    text_kv = lax.all_gather(text_kv, "vis", axis=0, tiled=True, axis_index_groups=QUADS)

    packed = response(qa, qb, text_kv, mask, vis_kv)
    back = lax.all_to_all(packed, "ctx", split_axis=0, concat_axis=0, tiled=True).astype(f32)
    levels = back[:, 256:258] + back[:, 258:260] + back[:, 260:262]
    levels = levels.reshape(N, 256)
    highest = jnp.maximum(jnp.max(levels, axis=0, keepdims=True), own_level)
    weights = jnp.exp(levels - highest)
    own_weight = jnp.exp(own_level - highest)
    total = jnp.sum(weights, axis=0, keepdims=True) + own_weight
    weights = weights / total
    own_weight = own_weight / total
    result = jnp.sum(back[:, :256] * weights[:, :, None], axis=0)
    result = result + own_mixed * own_weight.reshape(256, 1)
    result = jnp.transpose(result.reshape(2, R_TOK, HD), (1, 0, 2)).reshape(R_TOK, 256)
    live = (positions < resp_len[0])[:, None]
    result = jnp.where(live, result, 0.0).astype(bf16)
    top = lax.all_gather(result[:half], "vis", axis=1, tiled=True)
    bottom = lax.all_gather(result[half:], "vis", axis=1, tiled=True)
    return jnp.concatenate([top, bottom], axis=0)


def solution(mesh):
    return jax.shard_map(
        per_device,
        mesh=mesh,
        in_specs=(
            P(("ctx", "vis"), None),
            P(),
            P(None, "vis"),
            P("vis", None),
            P(),
            P(None, "vis"),
            P(),
            P(),
            P("ctx", "vis"),
            P("vis"),
            P("vis", None),
            P("ctx", None),
            P("ctx", None),
            P("ctx"),
        ),
        out_specs=P("ctx", None),
        check_vma=False,
    )
```

time: 635 us -> 336 us (0.53)
  waiting for transfers between devices: 379 us -> 86.2 us
  other arithmetic: 70.4 us -> 9.33 us
  Pallas kernels: 0 us -> 59.2 us
  matrix products: 42.8 us -> 4.46 us
  blocking collectives: 79.8 us -> 110 us
  starting transfers between devices: 11.7 us -> 30.6 us
  local copies, waits for them, and re-layouts: 35.3 us -> 21.6 us
    all_gather x5 -> x2, waiting for transfers between devices: 291 us -> 41.5 us  [the longest x1 39 us: per_device(): out_all = lax.all_gather(w_out, 'vis', axis=0)]
    all_gather x2 -> x6, blocking collectives: 36.8 us -> 110 us  [the longest x1 28.9 us: per_device(): lax.all_gather(text_kv, 'vis', axis=0, tiled=True, axis_index_groups=QUADS)]
    pallas_call x0 -> x3, Pallas kernels: none -> 59.2 us  [the longest x1 24.6 us: merge(): pl.pallas_call(merge_kernel, grid_spec=grid_spec, out_shape=jax.ShapeDtyp...]
    reduce_scatter x1, waiting for transfers between devices: 55.9 us -> 0.01 us  [per_device(): lax.psum_scatter(text_part, 'vis', scatter_dimension=0, tiled=True)]
    add x34 -> x2, other arithmetic: 41 us -> 0.02 us  [the longest x1 0.01 us: ring_owners(): return jnp.concatenate([zs * 2 + core, zs * 2 + 1 - core])]
    dot_general x18 -> x4, matrix products: 42.8 us -> 4.46 us  [the longest x2 2.56 us: dot(): lax.dot_general(a, b, ((contract[:1], contract[1:]), ((), ())), preferred...]
    ppermute x0 -> x9, waiting for transfers between devices: none -> 27.3 us  [the longest x3 22.5 us: ring_gather(): ups.append(lax.ppermute(ups[-1], 'vis', along_z(1)))]
    psum x1 -> x0, blocking collectives: 25.8 us -> none  [per_device(): squares = lax.psum(jnp.sum(prompt_floats * prompt_floats, axis=1), 'vis')]
  transfers between devices with their start and end apart: 8 -> 14, of which waited for: 7 -> 8; matrix products, arithmetic and copies ran while one was open for 7% -> 8% of each run, Pallas kernels for 0% -> 12%
where the time goes in v1:
time: 336 us; the launch traced here: 335 us
  blocking collectives  110 us (33%)
  waiting for transfers between devices  86.2 us (26%)
  Pallas kernels  59.2 us (18%)
  starting transfers between devices  30.6 us (9%)
  local copies, waits for them, and re-layouts  21.6 us (6%)
  between operations  14.2 us (4%)
  other arithmetic  9.33 us (3%)
  matrix products  4.46 us (1%)
    all_gather x1, waiting for transfers between devices, per_device(): out_all = lax.all_gather(w_out, 'vis', axis=0)  39 us
    all_gather x1, blocking collectives, per_device(): lax.all_gather(text_kv, 'vis', axis=0, tiled=True, axis_index_groups=QUADS)  28.9 us
    pallas_call x1, Pallas kernels, merge(): pl.pallas_call(merge_kernel, grid_spec=grid_spec, out_shape=jax.ShapeDtyp...  24.6 us
    ppermute x3, waiting for transfers between devices, ring_gather(): ups.append(lax.ppermute(ups[-1], 'vis', along_z(1)))  22.5 us
    all_gather x1, blocking collectives, per_device(): qa = lax.all_gather(own_q[:half], 'ctx', axis=0)  20.2 us
    all_gather x1, blocking collectives, per_device(): qb = lax.all_gather(own_q[half:], 'ctx', axis=0)  19.5 us
    all_gather x1, blocking collectives, per_device(): top = lax.all_gather(result[:half], 'vis', axis=1, tiled=True)  19.3 us
    pallas_call x1, Pallas kernels, response(): pl.pallas_call(response_kernel, grid=(N,), in_specs=[pl.BlockSpec((1, R_T...  18.9 us
  transfers between devices with their start and end apart: 14, of which 8 were waited for; matrix products, arithmetic and copies ran while one was open for 8% of the time, Pallas kernels for 12%

profile of v1, /device:TPU:1, one launch (start us, length us, event | category | flops | bytes accessed | tf_op | source)
XLA Modules:
  0.0 335.3 jit_solution(4259802149125539472)
XLA Ops:
  12.5 2.9 pad_maximum_fusion
  15.4 39.0 %all-gather.8.cloned.1.call-done = bf16[1280,1280]{1,0:T(8,128)(2,1)} async-done(((bf16[80,1280]{1,0:T(8,128)(2,1)}), bf16[1280,1280]{1,0:T(8,128)(2,1)}) %all-gather.8.cloned.1.call-update) | async-done | bytes 3276816 | tf_op jit(solution)/shard_map/all_gather | solution.py:288
  56.3 20.2 %all-gather = bf16[1024,256]{1,0:T(8,128)(2,1)S(1)} all-gather(bf16[64,256]{1,0:T(8,128)(2,1)S(1)} %copy.37), channel_id=2, replica_groups=mesh['ctx'=16,'vis'=16] {'ctx'}, dimensions={0}, use_global_device_ids=true | all-gather | bytes 557056 | tf_op jit(solution)/shard_map/all_gather | solution.py:253
  76.5 19.5 %all-gather.1 = bf16[1024,256]{1,0:T(8,128)(2,1)S(1)} all-gather(bf16[64,256]{1,0:T(8,128)(2,1)S(1)} %copy.38), channel_id=3, replica_groups=mesh['ctx'=16,'vis'=16] {'ctx'}, dimensions={0}, use_global_device_ids=true | all-gather | bytes 557056 | tf_op jit(solution)/shard_map/all_gather | solution.py:254
  96.0 2.5 all-gather.6.cloned.1.call-done.x_ref
  98.5 2.5 copy-done.1
  101.0 15.7 %vision.1 = bf16[80,2048]{1,0:T(8,128)(2,1)S(1)} custom-call(bf16[2048,1280]{1,0:T(8,128)(2,1)S(1)} %copy-done.1, f32[1,1280]{1,0:T(1,128)S(1)} %reshape.268.gain_ref, bf16[1280,384]{1,0:T(8,128)(2,1)S(1)} %copy.41.w_ref), custom_call_target="tpu_custom_call" | custom-call | tf_op jit(solution)/shard_map/vision/pallas_call | solution.py:98
  119.4 8.2 %collective-permute-done = bf16[80,2048]{1,0:T(8,128)(2,1)S(1)} collective-permute-done((bf16[80,2048]{1,0:T(8,128)(2,1)S(1)}, bf16[80,2048]{1,0:T(8,128)(2,1)S(1)}, u32[]{:S(2)}, u32[]{:S(2)}) %collective-permute-start) | collective-permute-done | bytes 327712 | tf_op jit(solution)/shard_map/ppermute | solution.py:41
  127.6 2.7 collective-permute-start.4
  131.3 7.0 %collective-permute-done.1 = bf16[80,2048]{1,0:T(8,128)(2,1)S(1)} collective-permute-done((bf16[80,2048]{1,0:T(8,128)(2,1)S(1)}, bf16[80,2048]{1,0:T(8,128)(2,1)S(1)}, u32[]{:S(2)}, u32[]{:S(2)}) %collective-permute-start.1) | collective-permute-done | bytes 327712 | tf_op jit(solution)/shard_map/ppermute | solution.py:41
  142.9 7.2 %collective-permute-done.2 = bf16[80,2048]{1,0:T(8,128)(2,1)S(1)} collective-permute-done((bf16[80,2048]{1,0:T(8,128)(2,1)S(1)}, bf16[80,2048]{1,0:T(8,128)(2,1)S(1)}, u32[]{:S(2)}, u32[]{:S(2)}) %collective-permute-start.2) | collective-permute-done | bytes 327712 | tf_op jit(solution)/shard_map/ppermute | solution.py:41
  150.3 3.0 collective-permute-start.7
  157.0 2.6 collective-permute-done.6
  161.1 8.4 %collective-permute-start.8 = (bf16[640,2048]{1,0:T(8,128)(2,1)}, bf16[640,2048]{1,0:T(8,128)(2,1)}, u32[]{:S(2)}, u32[]{:S(2)}) collective-permute-start(bf16[640,2048]{1,0:T(8,128)(2,1)} %get-tuple-element.35), channel_id=1, source_target_pairs={{0,1},{1,0},{2,3},{3,2},{4,5},{5,4},{6,7},{7,6},{8,9},{9,8},{10,11... | collective-permute-start | bytes 7864328 | tf_op jit(solution)/shard_map/ppermute | solution.py:47
  174.3 3.7 %constant_dynamic-update-slice_fusion.9.h_ref = bf16[1280,2048]{1,0:T(8,128)(2,1)} fusion(bf16[1280,2048]{1,0:T(8,128)(2,1)} %get-tuple-element.36, bf16[640,2048]{1,0:T(8,128)(2,1)} %collective-permute-done.8), kind=kLoop, calls=%fused_computation.50 | loop fusion | bytes 5242880 | tf_op jit(solution)/shard_map/concatenate | solution.py:47
  178.0 24.6 %merge.1 = bf16[16,72,512]{2,1,0:T(8,128)(2,1)} custom-call(s32[16]{0:T(128)} %pad_add_fusion.order_ref, bf16[1280,2048]{1,0:T(8,128)(2,1)} %constant_dynamic-update-slice_fusion.9.h_ref, bf16[2048,1280]{1,0:T(8,128)(2,1)} %all-gather.6.cloned.1.call-done.x_ref, bf16[16,80,1280]{2,1,0:T(8,128)(2,1)} %bitcast.78, f32[1,1280]{1,0:T(1,128)} %reshape.271.gain_ref, ...), custom_call_target="tpu_custom_call" | custom-call | tf_op jit(solution)/shard_map/merge/pallas_call | solution.py:167
  202.6 7.2 %all-to-all-start = ((bf16[16,72,512]{2,1,0:T(8,128)(2,1)}), bf16[16,72,512]{2,1,0:T(8,128)(2,1)}, u32[]{:S(2)}, u32[]{:S(2)}) async-start(bf16[16,72,512]{2,1,0:T(8,128)(2,1)} %merge.1), calls=%async_computation.1 | async-start | bytes 2359296 | tf_op jit(solution)/shard_map/all_to_all | solution.py:306
  212.9 28.9 %all_gather.40.text_ref = bf16[256,1024]{1,0:T(8,128)(2,1)S(1)} all-gather(bf16[64,1024]{1,0:T(8,128)(2,1)S(1)} %fusion.14), channel_id=1, replica_groups={{0,1,2,3},{4,5,6,7},{8,9,10,11},{12,13,14,15},{16,17,18,19},{20,21,22,2..., dimensions={0}, use_global_device_ids=true | all-gather | bytes 655360 | tf_op jit(solution)/shard_map/all_gather | solution.py:311
  243.3 5.9 %all_gather.41.vis_ref = bf16[256,512]{1,0:T(8,128)(2,1)S(1)} all-gather(bf16[64,512]{1,0:T(8,128)(2,1)S(1)} %fusion.15), channel_id=1, replica_groups={{0,1,2,3},{4,5,6,7},{8,9,10,11},{12,13,14,15},{16,17,18,19},{20,21,22,2..., dimensions={0}, use_global_device_ids=true | all-gather | bytes 327680 | tf_op jit(solution)/shard_map/all_gather | solution.py:310
  249.2 18.9 %response.1 = bf16[16,272,128]{2,1,0:T(8,128)(2,1)} custom-call(bf16[16,64,256]{2,1,0:T(8,128)(2,1)S(1)} %bitcast.69, bf16[16,64,256]{2,1,0:T(8,128)(2,1)S(1)} %bitcast.70, bf16[256,1024]{1,0:T(8,128)(2,1)S(1)} %all_gather.40.text_ref, f32[1,1024]{1,0:T(1,128)S(1)} %bitcast.71, bf16[256,512]{1,0:T(8,128)(2,1)S(1)} %all_gather.41.vis_ref), custom_call_target="tpu_custom_call" | custom-call | tf_op jit(solution)/shard_map/response/pallas_call | solution.py:211
  268.2 3.7 %all-to-all-start.1 = ((bf16[16,272,128]{2,1,0:T(8,128)(2,1)}), bf16[16,272,128]{2,1,0:T(8,128)(2,1)S(1)}, u32[]{:S(2)}, u32[]{:S(2)}) async-start(bf16[16,272,128]{2,1,0:T(8,128)(2,1)} %response.1), calls=%async_computation.2 | async-start | bytes 2228224 | tf_op jit(solution)/shard_map/all_to_all | solution.py:314
  273.6 16.6 %all-to-all-done.1 = bf16[16,272,128]{2,1,0:T(8,128)(2,1)S(1)} async-done(((bf16[16,272,128]{2,1,0:T(8,128)(2,1)}), bf16[16,272,128]{2,1,0:T(8,128)(2,1)S(1)}, u32[]{:S(2)}, u32[]{:S(2)}) %all-to-all-start.1) | async-done | bytes 1114144 | tf_op jit(solution)/shard_map/all_to_all | solution.py:314
  292.5 19.3 %all_gather.42 = bf16[64,4096]{1,0:T(8,128)(2,1)S(1)} all-gather(bf16[64,256]{1,0:T(8,128)(2,1)S(1)} %get-tuple-element.39), channel_id=1, replica_groups=mesh['ctx'=16,'vis'=16] {'vis'}, dimensions={1}, use_global_device_ids=true | all-gather | bytes 557056 | tf_op jit(solution)/shard_map/all_gather | solution.py:328
  311.8 15.9 %all_gather.43 = bf16[64,4096]{1,0:T(8,128)(2,1)S(1)} all-gather(bf16[64,256]{1,0:T(8,128)(2,1)S(1)} %get-tuple-element.40), channel_id=1, replica_groups=mesh['ctx'=16,'vis'=16] {'vis'}, dimensions={1}, use_global_device_ids=true | all-gather | bytes 557056 | tf_op jit(solution)/shard_map/all_gather | solution.py:329
  (102 shorter events, 35.0 us)
Async XLA Ops:
  6.5 48.0 %copy-start = (bf16[128,4096]{1,0:T(8,128)(2,1)S(1)}, bf16[128,4096]{1,0:T(8,128)(2,1)}, u32[]{:S(2)}) copy-start(bf16[128,4096]{1,0:T(8,128)(2,1)} %param.26) | copy-start | bytes 3145732
  6.5 47.9 %all-gather.8.cloned.1.call-start = ((), (), s32[]{:S(2)}) async-start(), calls=%async_computation.5 | async-start | bytes 3481600 | tf_op jit(solution)/shard_map/all_gather | solution.py:288
  7.3 91.2 %all-gather.6.cloned.1.call-start = ((), (), s32[]{:S(2)}) async-start(), calls=%async_computation.3 | async-start | bytes 5570560 | tf_op jit(solution)/shard_map/all_gather | solution.py:249
  8.4 2.5 copy-start.4
  9.2 1.9 copy-start.8
  9.2 202.0 %reduce-scatter.2.cloned.1.call-start = ((), (), s32[]{:S(2)}) async-start(), calls=%async_computation.4 | async-start | bytes 5013504 | tf_op jit(solution)/shard_map/reduce_scatter | solution.py:290
  54.5 1.8 copy-start.9
  98.5 2.5 copy-start.1
  116.6 11.0 %collective-permute-start = (bf16[80,2048]{1,0:T(8,128)(2,1)S(1)}, bf16[80,2048]{1,0:T(8,128)(2,1)S(1)}, u32[]{:S(2)}, u32[]{:S(2)}) collective-permute-start(bf16[80,2048]{1,0:T(8,128)(2,1)S(1)} %vision.1), channel_id=1, source_target_pairs={{0,2},{1,3},{2,4},{3,5},{4,6},{5,7},{6,8},{7,9},{8,10},{9,11},{10,... | collective-permute-start | bytes 983048 | tf_op jit(solution)/shard_map/ppermute | solution.py:41
  117.8 9.8 %collective-permute-start.3 = (bf16[80,2048]{1,0:T(8,128)(2,1)S(1)}, bf16[80,2048]{1,0:T(8,128)(2,1)S(1)}, u32[]{:S(2)}, u32[]{:S(2)}) collective-permute-start(bf16[80,2048]{1,0:T(8,128)(2,1)S(1)} %vision.1), channel_id=1, source_target_pairs={{0,14},{1,15},{2,0},{3,1},{4,2},{5,3},{6,4},{7,5},{8,6},{9,7},{10,... | collective-permute-start | bytes 983048 | tf_op jit(solution)/shard_map/ppermute | solution.py:42
  127.6 10.7 %collective-permute-start.1 = (bf16[80,2048]{1,0:T(8,128)(2,1)S(1)}, bf16[80,2048]{1,0:T(8,128)(2,1)S(1)}, u32[]{:S(2)}, u32[]{:S(2)}) collective-permute-start(bf16[80,2048]{1,0:T(8,128)(2,1)S(1)} %collective-permute-done), channel_id=1, source_target_pairs={{0,2},{1,3},{2,4},{3,5},{4,6},{5,7},{6,8},{7,9},{8,10},{9,11},{10,... | collective-permute-start | bytes 983048 | tf_op jit(solution)/shard_map/ppermute | solution.py:41
  127.6 11.1 %collective-permute-start.4 = (bf16[80,2048]{1,0:T(8,128)(2,1)S(1)}, bf16[80,2048]{1,0:T(8,128)(2,1)S(1)}, u32[]{:S(2)}, u32[]{:S(2)}) collective-permute-start(bf16[80,2048]{1,0:T(8,128)(2,1)S(1)} %collective-permute-done.3), channel_id=1, source_target_pairs={{0,14},{1,15},{2,0},{3,1},{4,2},{5,3},{6,4},{7,5},{8,6},{9,7},{10,... | collective-permute-start | bytes 983048 | tf_op jit(solution)/shard_map/ppermute | solution.py:42
  138.3 11.8 %collective-permute-start.2 = (bf16[80,2048]{1,0:T(8,128)(2,1)S(1)}, bf16[80,2048]{1,0:T(8,128)(2,1)S(1)}, u32[]{:S(2)}, u32[]{:S(2)}) collective-permute-start(bf16[80,2048]{1,0:T(8,128)(2,1)S(1)} %collective-permute-done.1), channel_id=1, source_target_pairs={{0,2},{1,3},{2,4},{3,5},{4,6},{5,7},{6,8},{7,9},{8,10},{9,11},{10,... | collective-permute-start | bytes 983048 | tf_op jit(solution)/shard_map/ppermute | solution.py:41
  138.7 11.5 %collective-permute-start.5 = (bf16[80,2048]{1,0:T(8,128)(2,1)S(1)}, bf16[80,2048]{1,0:T(8,128)(2,1)S(1)}, u32[]{:S(2)}, u32[]{:S(2)}) collective-permute-start(bf16[80,2048]{1,0:T(8,128)(2,1)S(1)} %collective-permute-done.4), channel_id=1, source_target_pairs={{0,14},{1,15},{2,0},{3,1},{4,2},{5,3},{6,4},{7,5},{8,6},{9,7},{10,... | collective-permute-start | bytes 983048 | tf_op jit(solution)/shard_map/ppermute | solution.py:42
  150.1 19.3 %copy-start.3 = (bf16[512,4,2,2,64]{0,4,3,2,1:T(8,128)(2,1)S(1)}, bf16[512,4,2,2,64]{0,4,3,2,1:T(8,128)(2,1)}, u32[]{:S(2)}) copy-start(bf16[512,4,2,2,64]{0,4,3,2,1:T(8,128)(2,1)} %copy-done.2) | copy-start | bytes 3145732
  150.1 9.4 %collective-permute-start.6 = (bf16[40,2048]{1,0:T(8,128)(2,1)S(1)}, bf16[40,2048]{1,0:T(8,128)(2,1)S(1)}, u32[]{:S(2)}, u32[]{:S(2)}) collective-permute-start(bf16[40,2048]{1,0:T(8,128)(2,1)S(1)} %slice.69), channel_id=1, source_target_pairs={{0,2},{1,3},{2,4},{3,5},{4,6},{5,7},{6,8},{7,9},{8,10},{9,11},{10,... | collective-permute-start | bytes 491528 | tf_op jit(solution)/shard_map/ppermute | solution.py:44
  150.3 10.0 %collective-permute-start.7 = (bf16[40,2048]{1,0:T(8,128)(2,1)S(1)}, bf16[40,2048]{1,0:T(8,128)(2,1)S(1)}, u32[]{:S(2)}, u32[]{:S(2)}) collective-permute-start(bf16[40,2048]{1,0:T(8,128)(2,1)S(1)} %slice.70), channel_id=1, source_target_pairs={{0,14},{1,15},{2,0},{3,1},{4,2},{5,3},{6,4},{7,5},{8,6},{9,7},{10,... | collective-permute-start | bytes 491528 | tf_op jit(solution)/shard_map/ppermute | solution.py:45
  155.1 15.7 %copy-start.10 = (f32[1280]{0:T(1024)S(1)}, f32[1280]{0:T(1024)}, u32[]{:S(2)}) copy-start(f32[1280]{0:T(1024)} %param.19) | copy-start | bytes 15364
  155.1 16.2 %copy-start.11 = (s32[8]{0:T(128)S(1)}, s32[8]{0:T(128)}, u32[]{:S(2)}) copy-start(s32[8]{0:T(128)} %constant.120) | copy-start | bytes 100
  161.1 13.2 %collective-permute-start.8 = (bf16[640,2048]{1,0:T(8,128)(2,1)}, bf16[640,2048]{1,0:T(8,128)(2,1)}, u32[]{:S(2)}, u32[]{:S(2)}) collective-permute-start(bf16[640,2048]{1,0:T(8,128)(2,1)} %get-tuple-element.35), channel_id=1, source_target_pairs={{0,1},{1,0},{2,3},{3,2},{4,5},{5,4},{6,7},{7,6},{8,9},{9,8},{10,11... | collective-permute-start | bytes 7864328 | tf_op jit(solution)/shard_map/ppermute | solution.py:47
  178.0 31.8 %copy-start.6 = (s32[16,512]{1,0:T(8,128)S(1)}, s32[16,512]{1,0:T(8,128)}, u32[]{:S(2)}) copy-start(s32[16,512]{1,0:T(8,128)} %param.21) | copy-start | bytes 98308
  178.0 31.8 %copy-start.7 = (s32[16,512]{1,0:T(8,128)S(1)}, s32[16,512]{1,0:T(8,128)}, u32[]{:S(2)}) copy-start(s32[16,512]{1,0:T(8,128)} %param.22) | copy-start | bytes 98308
  202.6 39.3 %all-to-all-start = ((bf16[16,72,512]{2,1,0:T(8,128)(2,1)}), bf16[16,72,512]{2,1,0:T(8,128)(2,1)}, u32[]{:S(2)}, u32[]{:S(2)}) async-start(bf16[16,72,512]{2,1,0:T(8,128)(2,1)} %merge.1), calls=%async_computation.1 | async-start | bytes 2359296 | tf_op jit(solution)/shard_map/all_to_all | solution.py:306
  268.2 22.0 %all-to-all-start.1 = ((bf16[16,272,128]{2,1,0:T(8,128)(2,1)}), bf16[16,272,128]{2,1,0:T(8,128)(2,1)S(1)}, u32[]{:S(2)}, u32[]{:S(2)}) async-start(bf16[16,272,128]{2,1,0:T(8,128)(2,1)} %response.1), calls=%async_computation.2 | async-start | bytes 2228224 | tf_op jit(solution)/shard_map/all_to_all | solution.py:314
  (2 other events, 2.7 us)
Sparse Core Ops, SparseCore 0:
  9.2 45.2 all-gather.7
  56.3 42.1 all-gather.5
  101.1 68.5 reduce-scatter.1
